TPU v7x, 128 devices: a whole 4x4x4 slice. The times are simulated.
128 devices in a mesh: gx: 16 (over z_lo, x, core), gy: 8 (over z_hi, y).
Axes of the slice: x: 4, y: 4, z: 4 (z_hi: 2, z_lo: 2; z = z_hi * 2 + z_lo), core: 2. Of those that a mesh axis runs over, the one named last changes fastest.
Arguments:
- adjoint_in: float32 [4, 72, 512, 1024], P(None, None, 'gx', 'gy'), may hold values from -6 to 6
- courant_x: float32 [72, 512, 1024], P(None, 'gx', 'gy'), may hold values from -0.9 to 0.9
- courant_y: float32 [72, 512, 1024], P(None, 'gx', 'gy'), may hold values from -0.9 to 0.9
- mixing: float32 [71, 512, 1024], P(None, 'gx', 'gy'), may hold values from 0.05 to 5
- kernel_rows: bfloat16 [72, 524288], P(None, ('gx', 'gy')), may hold values from -6 to 6
- tracer_weights: bfloat16 [4, 524288], P(None, ('gx', 'gy')), may hold values from 0.25 to 1.5
- column_ids: int32 [524288], P(('gx', 'gy')), may hold values from 0 to 4095
- counts: int32 [128, 128], P(('gx', 'gy')), may hold values from 0 to 32, as said below
Outputs:
- adjoint_out: float32 [4, 72, 512, 1024], P(None, None, 'gx', 'gy')
- flux_gradient: float32 [4, 512, 1024], P(None, 'gx', 'gy')
Inputs may be any that keep to these rules, and one draw needn't show every extreme that they name: `counts`: live slots from one device to another; 32 is reached by one receiving device from every sender. `column_ids`: column id in the receiving tile, longitude-major.
All inputs are finite; a program needn't handle non-finite values.
Results may differ from a plain program's by a relative error of at most 0.0003.
Values may be sent and summed in bfloat16 or wider, within the bound.
No kernel may reach another device: no remote copies, remote signals or barrier semaphores. Data moves between devices by JAX's collectives and lax.ppermute only.
A program may use at most 320 MiB of HBM per device.

v0:
```python
import jax
import jax.numpy as jnp
from jax import lax
from jax.sharding import PartitionSpec as P

STEPS = 2
first_coef = (0.75, -0.15, 1.0 / 60.0)
second_coef = (1.5, -0.15, 1.0 / 90.0)
second_center = -49.0 / 18.0


def extended(cells, sides, width, closed):
    for axis, dim in sides:
        count = lax.axis_size(axis)
        ends = count if closed else count - 1
        head = lax.slice_in_dim(cells, 0, width, axis=dim)
        tail = lax.slice_in_dim(cells, cells.shape[dim] - width, cells.shape[dim], axis=dim)
        cells = jnp.concatenate(
            [
                lax.ppermute(tail, axis, [(i, (i + 1) % count) for i in range(ends)]),
                cells,
                lax.ppermute(head, axis, [((i + 1) % count, i) for i in range(ends)]),
            ],
            axis=dim,
        )
    return cells


def advect(padded, courant, axis, length):

    def piece(offset):
        return lax.slice_in_dim(padded, 3 + offset, 3 + offset + length, axis=axis)

    center = piece(0)
    slope = first_coef[0] * (piece(1) - piece(-1))
    curve = second_center * center + second_coef[0] * (piece(1) + piece(-1))
    for shift_k in (2, 3):
        slope = slope + first_coef[shift_k - 1] * (piece(shift_k) - piece(-shift_k))
        curve = curve + second_coef[shift_k - 1] * (piece(shift_k) + piece(-shift_k))
    return center + courant * slope + 0.5 * courant * courant * curve


def factor(mixing):
    levels = mixing.shape[0] + 1
    cps = []
    invs = []
    for level in range(levels):
        diag_part = jnp.ones_like(mixing[0])
        if level > 0:
            diag_part = diag_part + mixing[level - 1]
        if level < levels - 1:
            diag_part = diag_part + mixing[level]
        if level > 0:
            diag_part = diag_part - mixing[level - 1] * cps[level - 1] * -1.0
        inverse = 1.0 / diag_part
        invs.append(inverse)
        if level < levels - 1:
            cps.append(-mixing[level] * inverse)
    return (cps, invs)


def solve(field, mixing, cps, invs):
    levels = len(invs)
    carry = field[..., 0, :, :] * invs[0]
    forward = [carry]
    for level in range(1, levels):
        carry = (field[..., level, :, :] + mixing[level - 1] * carry) * invs[level]
        forward.append(carry)
    result = [None] * levels
    result[levels - 1] = forward[levels - 1]
    for level in range(levels - 2, -1, -1):
        result[level] = forward[level] - cps[level] * result[level + 1]
    return jnp.stack(result, axis=-3)


def local(
    adjoint_in, courant_x, courant_y, mixing, kernel_rows, tracer_weights, column_ids, counts
):
    tracer_count, level_count, lon_cells, lat_cells = adjoint_in.shape
    devices = lax.axis_size(("gx", "gy"))
    slot_count = kernel_rows.shape[1] // devices
    slot_place = jnp.arange(devices * slot_count, dtype=jnp.int32) % slot_count
    limits = jnp.repeat(counts[0], slot_count, total_repeat_length=devices * slot_count)
    live_rows = jnp.where((slot_place < limits)[None, :], kernel_rows, jnp.zeros_like(kernel_rows))
    got_rows, got_weights = (
        lax.all_to_all(live_rows, ("gx", "gy"), split_axis=1, concat_axis=1, tiled=True),
        lax.all_to_all(tracer_weights, ("gx", "gy"), split_axis=1, concat_axis=1, tiled=True),
    )
    cell_range = jnp.arange(lon_cells * lat_cells, dtype=jnp.int32)
    onehot = (column_ids[:, None] == cell_range[None, :]).astype(jnp.bfloat16)
    forcing_list = []
    for tracer in range(tracer_count):
        placed = onehot * got_weights[tracer][:, None]
        forcing_list.append(jnp.dot(got_rows, placed, preferred_element_type=jnp.float32))
    forcing = jnp.stack(forcing_list, axis=0)
    state = adjoint_in + forcing.reshape(tracer_count, level_count, lon_cells, lat_cells)
    cps, invs = factor(mixing)
    gradient = jnp.zeros((tracer_count, lon_cells, lat_cells), jnp.float32)
    for step in range(STEPS):
        wrapped = extended(state, (("gx", 2),), 3, True)
        zonal = advect(wrapped, courant_x, 2, lon_cells)
        padded = extended(zonal, (("gy", 3),), 3, False)
        meridional = advect(padded, courant_y, 3, lat_cells)
        state = solve(meridional, mixing, cps, invs)
        gradient = gradient + state[:, 0]
    return (state, gradient)


def solution(mesh):
    in_specs = (
        P(None, None, "gx", "gy"),
        P(None, "gx", "gy"),
        P(None, "gx", "gy"),
        P(None, "gx", "gy"),
        P(None, ("gx", "gy")),
        P(None, ("gx", "gy")),
        P(("gx", "gy")),
        P(("gx", "gy"), None),
    )
    out_specs = (P(None, None, "gx", "gy"), P(None, "gx", "gy"))
    return jax.shard_map(local, mesh=mesh, in_specs=in_specs, out_specs=out_specs, check_vma=False)
```

profile of v0, /device:TPU:64, one launch (start us, length us, event | category | flops | bytes accessed | tf_op | source)
XLA Modules:
  0.0 418.8 jit_solution(15522353103420576083)
XLA Ops:
  2.3 10.0 %all-to-all-start.1 = ((bf16[4,128,32]{2,0,1:T(4,128)(2,1)}), bf16[4,128,32]{2,0,1:T(4,128)(2,1)S(1)}, u32[]{:S(2)}, u32[]{:S(2)}) async-start(bf16[4,128,32]{2,0,1:T(4,128)(2,1)} %copy.1397), calls=%async_computation.1 | async-start | bytes 262144 | tf_op jit(solution)/shard_map/all_to_all | solution.py:87
  17.0 24.7 %gather_fusion = s32[4096]{0:T(1024)S(1)} fusion(s32[128]{0:T(128)S(1)} %bitcast.3716, s32[4096]{0:T(1024)S(1)} %broadcast_clamp_fusion), kind=kCustom, calls=%fused_computation | custom fusion | bytes 49152 | tf_op jit(solution)/shard_map/jit(_take)/gather | solution.py:83
  66.1 10.6 %all-to-all-start = ((bf16[72,128,32]{0,2,1:T(8,128)(2,1)}), bf16[72,128,32]{0,2,1:T(8,128)(2,1)}, u32[]{:S(2)}, u32[]{:S(2)}) async-start(bf16[72,128,32]{0,2,1:T(8,128)(2,1)} %bitcast.6), calls=%async_computation | async-start | bytes 2097152 | tf_op jit(solution)/shard_map/all_to_all | solution.py:86
  86.3 7.5 %all-to-all-done = bf16[72,128,32]{0,2,1:T(8,128)(2,1)} async-done(((bf16[72,128,32]{0,2,1:T(8,128)(2,1)}), bf16[72,128,32]{0,2,1:T(8,128)(2,1)}, u32[]{:S(2)}, u32[]{:S(2)}) %all-to-all-start) | async-done | bytes 589856 | tf_op jit(solution)/shard_map/all_to_all | solution.py:86
  93.8 13.3 %fusion.3 = f32[72,32,128]{2,0,1:T(8,128)S(1)} fusion(bf16[72,4096,1]{0,1,2:T(8,128)(2,1)} %bitcast.8, s32[32,128]{1,0:T(8,128)} %multiply_add_fusion.4, s32[4096]{0:T(1024)} %param.16, bf16[4096]{0:T(1024)(128)(2,1)} %mul.20172), kind=kOutput, calls=%fused_computation.8 | convolution fusion | flops 2449473536 | bytes 1810432 | tf_op jit(solution)/shard_map/dot_general | solution.py:94
  107.2 13.1 %fusion.2 = f32[72,32,128]{2,0,1:T(8,128)S(1)} fusion(bf16[72,4096,1]{0,1,2:T(8,128)(2,1)} %bitcast.8, s32[32,128]{1,0:T(8,128)S(1)} %copy-done.212, s32[4096]{0:T(1024)S(1)} %copy-done.216, bf16[4096]{0:T(1024)(128)(2,1)S(1)} %copy-done.213), kind=kOutput, calls=%fused_computation.7 | convolution fusion | flops 2449473536 | bytes 1810432 | tf_op jit(solution)/shard_map/dot_general | solution.py:94
  120.3 13.3 %fusion.1 = f32[72,32,128]{2,0,1:T(8,128)S(1)} fusion(bf16[72,4096,1]{0,1,2:T(8,128)(2,1)} %bitcast.8, s32[32,128]{1,0:T(8,128)S(1)} %copy-done.212, s32[4096]{0:T(1024)S(1)} %copy-done.216, bf16[4096]{0:T(1024)(128)(2,1)S(1)} %copy-done.214), kind=kOutput, calls=%fused_computation.6 | convolution fusion | flops 2449473536 | bytes 1810432 | tf_op jit(solution)/shard_map/dot_general | solution.py:94
  133.6 13.2 %fusion = f32[72,32,128]{2,0,1:T(8,128)S(1)} fusion(bf16[72,4096,1]{0,1,2:T(8,128)(2,1)} %bitcast.8, s32[32,128]{1,0:T(8,128)S(1)} %copy-done.212, s32[4096]{0:T(1024)S(1)} %copy-done.216, bf16[4096]{0:T(1024)(128)(2,1)S(1)} %mul.20163), kind=kOutput, calls=%fused_computation.5 | convolution fusion | flops 2449473536 | bytes 1810432 | tf_op jit(solution)/shard_map/dot_general | solution.py:94
  161.0 6.4 %multiply_add_fusion.3 = f32[4,72,32,128]{3,2,0,1:T(8,128)S(1)} fusion(f32[4,72,32,128]{3,2,0,1:T(8,128)S(1)} %maximum_add_fusion, f32[4,72,3,128]{3,2,0,1:T(4,128)S(1)} %copy.1408, f32[4,72,3,128]{3,2,0,1:T(4,128)S(1)} %copy.1410, f32[72,32,128]{2,1,0:T(8,128)S(1)} %multiply_multiply_fusion.1, f32[72,32,128]{2,1,0:T(8,128)S(1)} %copy-done.6), kind=kLoop, calls=%fused_computation.94 | loop fusion | flops 33030144 | bytes 12681216 | tf_op jit(solution)/shard_map/add | solution.py:40
  167.5 5.4 %fusion.559 = (f32[4,72,32,3]{3,2,0,1:T(8,128)}, f32[4,72,32,3]{3,2,0,1:T(8,128)}) fusion(f32[4,72,32,128]{3,2,0,1:T(8,128)S(1)} %multiply_add_fusion.3), kind=kLoop, calls=%fused_computation.1324 | loop fusion | bytes 442368 | tf_op jit(solution)/shard_map/slice | solution.py:17
  187.2 8.2 %collective-permute-done.3 = f32[4,72,32,3]{1,2,3,0:T(8,128)S(1)} collective-permute-done((f32[4,72,32,3]{1,2,3,0:T(8,128)S(1)}, f32[4,72,32,3]{1,2,3,0:T(8,128)S(1)}, u32[]{:S(2)}, u32[]{:S(2)}) %collective-permute-start.3) | collective-permute-done | bytes 110624 | tf_op jit(solution)/shard_map/ppermute | solution.py:20
  195.4 5.0 %copy.1414 = f32[4,72,32,3]{3,2,0,1:T(8,128)} copy(f32[4,72,32,3]{1,2,3,0:T(8,128)S(1)} %collective-permute-done.3) | data formatting | bytes 221184 | tf_op jit(solution)/shard_map/ppermute | solution.py:20
  200.4 5.1 %copy.1412 = f32[4,72,32,3]{3,2,0,1:T(8,128)} copy(f32[4,72,32,3]{1,2,3,0:T(8,128)S(1)} %collective-permute-done.2) | data formatting | bytes 221184 | tf_op jit(solution)/shard_map/ppermute | solution.py:22
  205.8 32.6 %multiply_add_fusion.2 = f32[4,72,32,128]{3,2,0,1:T(8,128)S(1)} fusion(f32[4,72,32,128]{3,2,0,1:T(8,128)} %copy-done.3, f32[4,72,32,3]{3,2,0,1:T(8,128)} %copy.1412, f32[4,72,32,3]{3,2,0,1:T(8,128)} %copy.1414, f32[72,32,128]{2,1,0:T(8,128)S(1)} %copy-done.11, f32[72,32,128]{2,1,0:T(8,128)S(1)} %copy-done.9), kind=kLoop, calls=%fused_computation.93 | loop fusion | flops 33030144 | bytes 12017664 | tf_op jit(solution)/shard_map/add | solution.py:40
  263.9 6.9 %collective-permute-done.5 = f32[4,72,3,128]{3,1,2,0:T(8,128)S(1)} collective-permute-done((f32[4,72,3,128]{3,1,2,0:T(8,128)S(1)}, f32[4,72,3,128]{3,1,2,0:T(8,128)S(1)}, u32[]{:S(2)}, u32[]{:S(2)}) %collective-permute-start.5) | collective-permute-done | bytes 442400 | tf_op jit(solution)/shard_map/ppermute | solution.py:20
  271.2 22.3 %add_multiply_fusion.5 = (f32[4,72,32,128]{3,2,0,1:T(8,128)}, f32[4,72,32,128]{3,2,0,1:T(8,128)}, f32[4,72,32,128]{3,2,0,1:T(8,128)}, f32[4,72,32,128]{3,2,0,1:T(8,128)}) fusion(f32[4,72,35,128]{3,2,0,1:T(8,128)S(1)} %copy_dynamic-update-slice_fusion, f32[4,72,32,128]{3,2,0,1:T(8,128)} %get-tuple-element.305, f32[4,72,3,128]{3,2,0,1:T(4,128)S(1)} %copy.1522, ...), kind=kLoop, calls=%fused_computation.91 | loop fusion | flops 24772608 | bytes 39370752 | tf_op jit(solution)/shard_map/mul | solution.py:36
  293.5 9.6 %copy_add_fusion.4 = f32[4,72,32,128]{3,2,1,0:T(8,128)S(1)} fusion(f32[4,72,32,128]{3,2,0,1:T(8,128)} %get-tuple-element.298, f32[4,72,32,128]{3,2,0,1:T(8,128)} %get-tuple-element.297, f32[4,72,32,128]{3,2,0,1:T(8,128)} %get-tuple-element.299, f32[4,72,32,128]{3,2,0,1:T(8,128)} %get-tuple-element.296, f32[4,72,32,128]{3,2,1,0:T(8,128)} %copy-done.4, ...), kind=kLoop, calls=%fused_computation.80 | loop fusion | flops 7077888 | bytes 29491200 | tf_op jit(solution)/shard_map/add | solution.py:40
  303.1 5.4 %fusion.557 = (f32[4,72,32,3]{3,2,1,0:T(8,128)}, f32[4,72,32,3]{3,2,1,0:T(8,128)}) fusion(f32[4,72,32,128]{3,2,1,0:T(8,128)S(1)} %copy_add_fusion.4), kind=kLoop, calls=%fused_computation.1322 | loop fusion | bytes 442368 | tf_op jit(solution)/shard_map/slice | solution.py:17
  318.4 7.5 %collective-permute-start.6 = (f32[4,72,32,3]{1,2,3,0:T(8,128)S(1)}, f32[4,72,32,3]{1,2,3,0:T(8,128)S(1)}, u32[]{:S(2)}, u32[]{:S(2)}) collective-permute-start(f32[4,72,32,3]{1,2,3,0:T(8,128)S(1)} %copy.1531), channel_id=1, source_target_pairs={{1,0},{2,1},{3,2},{4,3},{5,4},{6,5},{7,6},{9,8},{10,9},{11,10},{12... | collective-permute-start | bytes 331784 | tf_op jit(solution)/shard_map/ppermute | solution.py:22
  325.9 5.2 %copy.1537 = f32[4,72,32,128]{3,2,0,1:T(8,128)} copy(f32[4,72,32,128]{3,2,1,0:T(8,128)} %copy-done.2) | data formatting | bytes 9437184 | tf_op jit(solution)/shard_map/add | solution.py:40
  331.2 5.2 %copy.1535 = f32[4,72,32,3]{3,2,0,1:T(8,128)} copy(f32[4,72,32,3]{1,2,3,0:T(8,128)S(1)} %collective-permute-done.7) | data formatting | bytes 221184 | tf_op jit(solution)/shard_map/ppermute | solution.py:20
  336.4 4.9 %copy.1533 = f32[4,72,32,3]{3,2,0,1:T(8,128)} copy(f32[4,72,32,3]{1,2,3,0:T(8,128)S(1)} %collective-permute-done.6) | data formatting | bytes 221184 | tf_op jit(solution)/shard_map/ppermute | solution.py:22
  341.4 45.7 %add_multiply_fusion.2 = (f32[4,72,32,128]{3,2,0,1:T(8,128)}, f32[4,72,32,128]{3,2,0,1:T(8,128)}, f32[4,72,32,128]{3,2,0,1:T(8,128)}) fusion(f32[4,72,32,3]{3,2,0,1:T(8,128)} %copy.1533, f32[4,72,32,128]{3,2,0,1:T(8,128)} %copy.1537, f32[4,72,32,3]{3,2,0,1:T(8,128)} %copy.1535, f32[72,32,128]{2,1,0:T(8,128)S(1)} %copy-done.10), kind=kLoop, calls=%fused_computation.87 | loop fusion | flops 25952256 | bytes 20275200 | tf_op jit(solution)/shard_map/mul | solution.py:36
  387.4 11.0 %copy_add_fusion = f32[4,72,32,128]{3,2,1,0:T(8,128)S(1)} fusion(f32[4,72,32,128]{3,2,0,1:T(8,128)} %get-tuple-element.294, f32[4,72,32,128]{3,2,0,1:T(8,128)} %get-tuple-element.295, f32[4,72,32,128]{3,2,0,1:T(8,128)} %get-tuple-element.293, f32[4,72,32,128]{3,2,1,0:T(8,128)S(1)} %bitcast.3718, f32[72,32,128]{2,1,0:T(8,128)S(1)} %copy-done.12, ...), kind=kLoop, calls=%fused_computation.75 | loop fusion | flops 11796480 | bytes 29712384 | tf_op jit(solution)/shard_map/add | solution.py:40
  (680 shorter events, 121.4 us)
Async XLA Ops:
  2.3 63.8 %all-to-all-start.1 = ((bf16[4,128,32]{2,0,1:T(4,128)(2,1)}), bf16[4,128,32]{2,0,1:T(4,128)(2,1)S(1)}, u32[]{:S(2)}, u32[]{:S(2)}) async-start(bf16[4,128,32]{2,0,1:T(4,128)(2,1)} %copy.1397), calls=%async_computation.1 | async-start | bytes 262144 | tf_op jit(solution)/shard_map/all_to_all | solution.py:87
  16.2 42.6 %copy-start.50 = (f32[32,128]{1,0:T(8,128)}, f32[32,128]{1,0:T(8,128)S(1)}, u32[]{:S(2)}) copy-start(f32[32,128]{1,0:T(8,128)S(1)} %get-tuple-element.201) | copy-start | bytes 49156
  66.1 27.7 %all-to-all-start = ((bf16[72,128,32]{0,2,1:T(8,128)(2,1)}), bf16[72,128,32]{0,2,1:T(8,128)(2,1)}, u32[]{:S(2)}, u32[]{:S(2)}) async-start(bf16[72,128,32]{0,2,1:T(8,128)(2,1)} %bitcast.6), calls=%async_computation | async-start | bytes 2097152 | tf_op jit(solution)/shard_map/all_to_all | solution.py:86
  78.1 82.9 %copy-start.7 = (f32[72,32,128]{2,1,0:T(8,128)}, f32[72,32,128]{2,1,0:T(8,128)S(1)}, u32[]{:S(2)}) copy-start(f32[72,32,128]{2,1,0:T(8,128)S(1)} %multiply_multiply_fusion.1) | copy-start | bytes 3538948
  149.5 7.1 %collective-permute-start = (f32[4,72,3,128]{3,1,2,0:T(8,128)S(1)}, f32[4,72,3,128]{3,1,2,0:T(8,128)S(1)}, u32[]{:S(2)}, u32[]{:S(2)}) collective-permute-start(f32[4,72,3,128]{3,1,2,0:T(8,128)S(1)} %copy.1407), channel_id=1, source_target_pairs={{8,0},{16,8},{24,16},{32,24},{40,32},{48,40},{56,48},{64,56},{72,6... | collective-permute-start | bytes 1327112 | tf_op jit(solution)/shard_map/ppermute | solution.py:22
  150.8 10.0 %collective-permute-start.1 = (f32[4,72,3,128]{3,1,2,0:T(8,128)S(1)}, f32[4,72,3,128]{3,1,2,0:T(8,128)S(1)}, u32[]{:S(2)}, u32[]{:S(2)}) collective-permute-start(f32[4,72,3,128]{3,1,2,0:T(8,128)S(1)} %copy.1409), channel_id=1, source_target_pairs={{0,8},{8,16},{16,24},{24,32},{32,40},{40,48},{48,56},{56,64},{64,7... | collective-permute-start | bytes 1327112 | tf_op jit(solution)/shard_map/ppermute | solution.py:20
  180.9 19.5 %collective-permute-start.2 = (f32[4,72,32,3]{1,2,3,0:T(8,128)S(1)}, f32[4,72,32,3]{1,2,3,0:T(8,128)S(1)}, u32[]{:S(2)}, u32[]{:S(2)}) collective-permute-start(f32[4,72,32,3]{1,2,3,0:T(8,128)S(1)} %copy.1411), channel_id=1, source_target_pairs={{1,0},{2,1},{3,2},{4,3},{5,4},{6,5},{7,6},{9,8},{10,9},{11,10},{12... | collective-permute-start | bytes 331784 | tf_op jit(solution)/shard_map/ppermute | solution.py:22
  184.2 11.2 %collective-permute-start.3 = (f32[4,72,32,3]{1,2,3,0:T(8,128)S(1)}, f32[4,72,32,3]{1,2,3,0:T(8,128)S(1)}, u32[]{:S(2)}, u32[]{:S(2)}) collective-permute-start(f32[4,72,32,3]{1,2,3,0:T(8,128)S(1)} %copy.1413), channel_id=1, source_target_pairs={{0,1},{1,2},{2,3},{3,4},{4,5},{5,6},{6,7},{8,9},{9,10},{10,11},{11... | collective-permute-start | bytes 331784 | tf_op jit(solution)/shard_map/ppermute | solution.py:20
  187.1 51.3 %copy-start.204 = (f32[32,128]{1,0:T(8,128)}, f32[32,128]{1,0:T(8,128)S(1)}, u32[]{:S(2)}) copy-start(f32[32,128]{1,0:T(8,128)S(1)} %get-tuple-element.503) | copy-start | bytes 49156
  187.1 53.5 %copy-start.192 = (f32[32,128]{1,0:T(8,128)}, f32[32,128]{1,0:T(8,128)S(1)}, u32[]{:S(2)}) copy-start(f32[32,128]{1,0:T(8,128)S(1)} %get-tuple-element.504) | copy-start | bytes 49156
  187.1 53.5 %copy-start.202 = (f32[32,128]{1,0:T(8,128)}, f32[32,128]{1,0:T(8,128)S(1)}, u32[]{:S(2)}) copy-start(f32[32,128]{1,0:T(8,128)S(1)} %get-tuple-element.356) | copy-start | bytes 49156
  187.1 53.5 %copy-start.203 = (f32[32,128]{1,0:T(8,128)}, f32[32,128]{1,0:T(8,128)S(1)}, u32[]{:S(2)}) copy-start(f32[32,128]{1,0:T(8,128)S(1)} %get-tuple-element.502) | copy-start | bytes 49156
  187.1 60.7 %copy-start.135 = (f32[32,128]{1,0:T(8,128)}, f32[32,128]{1,0:T(8,128)S(1)}, u32[]{:S(2)}) copy-start(f32[32,128]{1,0:T(8,128)S(1)} %get-tuple-element.357) | copy-start | bytes 49156
  187.1 60.7 %copy-start.137 = (f32[32,128]{1,0:T(8,128)}, f32[32,128]{1,0:T(8,128)S(1)}, u32[]{:S(2)}) copy-start(f32[32,128]{1,0:T(8,128)S(1)} %get-tuple-element.501) | copy-start | bytes 49156
  205.5 33.0 %copy-start.19 = (f32[1,32,128]{2,1,0:T(8,128)S(1)}, f32[1,32,128]{2,1,0:T(8,128)}, u32[]{:S(2)}) copy-start(f32[1,32,128]{2,1,0:T(8,128)} %copy-done.18) | copy-start | bytes 49156
  205.5 33.0 %copy-start.21 = (f32[1,32,128]{2,1,0:T(8,128)S(1)}, f32[1,32,128]{2,1,0:T(8,128)}, u32[]{:S(2)}) copy-start(f32[1,32,128]{2,1,0:T(8,128)} %copy-done.20) | copy-start | bytes 49156
  205.5 33.0 %copy-start.23 = (f32[1,32,128]{2,1,0:T(8,128)S(1)}, f32[1,32,128]{2,1,0:T(8,128)}, u32[]{:S(2)}) copy-start(f32[1,32,128]{2,1,0:T(8,128)} %copy-done.22) | copy-start | bytes 49156
  259.6 11.3 %collective-permute-start.4 = (f32[4,72,3,128]{3,1,2,0:T(8,128)S(1)}, f32[4,72,3,128]{3,1,2,0:T(8,128)S(1)}, u32[]{:S(2)}, u32[]{:S(2)}) collective-permute-start(f32[4,72,3,128]{3,1,2,0:T(8,128)S(1)} %copy.1518), channel_id=1, source_target_pairs={{8,0},{16,8},{24,16},{32,24},{40,32},{48,40},{56,48},{64,56},{72,6... | collective-permute-start | bytes 1327112 | tf_op jit(solution)/shard_map/ppermute | solution.py:22
  260.9 9.8 %collective-permute-start.5 = (f32[4,72,3,128]{3,1,2,0:T(8,128)S(1)}, f32[4,72,3,128]{3,1,2,0:T(8,128)S(1)}, u32[]{:S(2)}, u32[]{:S(2)}) collective-permute-start(f32[4,72,3,128]{3,1,2,0:T(8,128)S(1)} %copy.1521), channel_id=1, source_target_pairs={{0,8},{8,16},{16,24},{24,32},{32,40},{40,48},{48,56},{56,64},{64,7... | collective-permute-start | bytes 1327112 | tf_op jit(solution)/shard_map/ppermute | solution.py:20
  312.5 18.7 %collective-permute-start.7 = (f32[4,72,32,3]{1,2,3,0:T(8,128)S(1)}, f32[4,72,32,3]{1,2,3,0:T(8,128)S(1)}, u32[]{:S(2)}, u32[]{:S(2)}) collective-permute-start(f32[4,72,32,3]{1,2,3,0:T(8,128)S(1)} %copy.1534), channel_id=1, source_target_pairs={{0,1},{1,2},{2,3},{3,4},{4,5},{5,6},{6,7},{8,9},{9,10},{10,11},{11... | collective-permute-start | bytes 331784 | tf_op jit(solution)/shard_map/ppermute | solution.py:20
  318.4 18.0 %collective-permute-start.6 = (f32[4,72,32,3]{1,2,3,0:T(8,128)S(1)}, f32[4,72,32,3]{1,2,3,0:T(8,128)S(1)}, u32[]{:S(2)}, u32[]{:S(2)}) collective-permute-start(f32[4,72,32,3]{1,2,3,0:T(8,128)S(1)} %copy.1531), channel_id=1, source_target_pairs={{1,0},{2,1},{3,2},{4,3},{5,4},{6,5},{7,6},{9,8},{10,9},{11,10},{12... | collective-permute-start | bytes 331784 | tf_op jit(solution)/shard_map/ppermute | solution.py:22
  336.4 50.7 %slice-start = ((s8[4718592]{0:T(1024)(128)(4,1)}), s8[524288]{0:T(1024)(128)(4,1)S(1)}, s32[]{:S(2)}) async-start(s8[4718592]{0:T(1024)(128)(4,1)} %bitcast.3717), calls=%async_computation.2 | async-start | bytes 1048576
  341.3 45.7 %slice-start.1 = ((s8[4718592]{0:T(1024)(128)(4,1)}), s8[4194304]{0:T(1024)(128)(4,1)S(1)}, s32[]{:S(2)}) async-start(s8[4718592]{0:T(1024)(128)(4,1)} %bitcast.3717), calls=%async_computation.3 | async-start | bytes 8388608
  341.4 45.7 %copy-start.12 = (f32[72,32,128]{2,1,0:T(8,128)S(1)}, f32[72,32,128]{2,1,0:T(8,128)}, u32[]{:S(2)}) copy-start(f32[72,32,128]{2,1,0:T(8,128)} %multiply_multiply_fusion) | copy-start | bytes 3538948
  (207 other events, 2708.7 us)
where the time goes:
time: 425 us; the launch traced here: 419 us
  other arithmetic  194 us (46%)
  local copies, waits for them, and re-layouts  97.1 us (23%)
  matrix products  52.9 us (12%)
  starting transfers between devices  38.9 us (9%)
  waiting for transfers between devices  30.4 us (7%)
  between operations  5.31 us (1%)
    mul x2, other arithmetic, advect(): curve = second_center * center + second_coef[0] * (piece(1) + piece(-1))  68 us
    add x4, other arithmetic, advect(): return center + courant * slope + 0.5 * courant * courant * curve  59.5 us
    dot_general x4, matrix products, local(): jnp.dot(got_rows, placed, preferred_element_type=jnp.float32)  52.9 us
    unnamed x75, other arithmetic  27 us
    gather x1, local copies, waits for them, and re-layouts, local(): jnp.repeat(counts[0], slot_count, total_repeat_length=devices * slot_count)  24.7 us
    slice x8, local copies, waits for them, and re-layouts, extended(): lax.slice_in_dim(cells, cells.shape[dim] - width, cells.shape[dim], axis=...  19.4 us
    ppermute x4, waiting for transfers between devices, extended(): lax.ppermute(tail, axis, [(i, (i + 1) % count) for i in range(ends)])  19.1 us
    ppermute x4, starting transfers between devices, extended(): lax.ppermute(head, axis, [((i + 1) % count, i) for i in range(ends)])  13.4 us
  transfers between devices with their start and end apart: 10, of which 5 were waited for; matrix products, arithmetic and copies ran while one was open for 21% of the time, Pallas kernels for 0%

commit v1 on v0

--- a/solution.py
+++ b/solution.py
@@ -7,6 +7,12 @@
 first_coef = (0.75, -0.15, 1.0 / 60.0)
 second_coef = (1.5, -0.15, 1.0 / 90.0)
 second_center = -49.0 / 18.0
+
+
+def stacked_exchange(x, mesh_axis, split, join):
+    pieces = jnp.split(x, lax.axis_size(mesh_axis), axis=split)
+    received = lax.all_to_all(jnp.stack(pieces), mesh_axis, 0, 0)
+    return jnp.concatenate(received, axis=join)
 
 
 def extended(cells, sides, width, closed):
@@ -84,7 +90,7 @@
     live_rows = jnp.where((slot_place < limits)[None, :], kernel_rows, jnp.zeros_like(kernel_rows))
     got_rows, got_weights = (
         lax.all_to_all(live_rows, ("gx", "gy"), split_axis=1, concat_axis=1, tiled=True),
-        lax.all_to_all(tracer_weights, ("gx", "gy"), split_axis=1, concat_axis=1, tiled=True),
+        stacked_exchange(tracer_weights, ("gx", "gy"), 1, 1),
     )
     cell_range = jnp.arange(lon_cells * lat_cells, dtype=jnp.int32)
     onehot = (column_ids[:, None] == cell_range[None, :]).astype(jnp.bfloat16)

time: 425 us -> 593 us (1.40)
  local copies, waits for them, and re-layouts: 97.1 us -> 262 us
    unnamed x512 -> x639, local copies, waits for them, and re-layouts: 6.58 us -> 172 us
  transfers between devices with their start and end apart: 10 -> 10, of which waited for: 5 -> 5; matrix products, arithmetic and copies ran while one was open for 21% -> 15% of each run, Pallas kernels for 0% -> 0%
where the time goes in v1:
time: 593 us; the launch traced here: 584 us
  local copies, waits for them, and re-layouts  262 us (44%)
  other arithmetic  194 us (33%)
  matrix products  52.9 us (9%)
  starting transfers between devices  38.9 us (7%)
  waiting for transfers between devices  30.4 us (5%)
    unnamed x639, local copies, waits for them, and re-layouts  172 us
    mul x2, other arithmetic, advect(): curve = second_center * center + second_coef[0] * (piece(1) + piece(-1))  68 us
    add x4, other arithmetic, advect(): return center + courant * slope + 0.5 * courant * courant * curve  59.5 us
    dot_general x4, matrix products, local(): jnp.dot(got_rows, placed, preferred_element_type=jnp.float32)  52.9 us
    unnamed x75, other arithmetic  27 us
    gather x1, local copies, waits for them, and re-layouts, local(): jnp.repeat(counts[0], slot_count, total_repeat_length=devices * slot_count)  24.7 us
    slice x8, local copies, waits for them, and re-layouts, extended(): lax.slice_in_dim(cells, cells.shape[dim] - width, cells.shape[dim], axis=...  19.4 us
    ppermute x4, waiting for transfers between devices, extended(): lax.ppermute(tail, axis, [(i, (i + 1) % count) for i in range(ends)])  19.1 us
  transfers between devices with their start and end apart: 10, of which 5 were waited for; matrix products, arithmetic and copies ran while one was open for 15% of the time, Pallas kernels for 0%

profile of v1, /device:TPU:64, one launch (start us, length us, event | category | flops | bytes accessed | tf_op | source)
XLA Modules:
  0.0 584.0 jit_solution(5589217764649513738)
XLA Ops:
  167.6 10.0 %all-to-all-start.1 = ((bf16[128,4,32]{2,1,0:T(4,128)(2,1)}), bf16[128,4,32]{2,1,0:T(4,128)(2,1)S(1)}, u32[]{:S(2)}, u32[]{:S(2)}) async-start(bf16[128,4,32]{2,1,0:T(4,128)(2,1)} %constant_dynamic-update-slice_fusion), calls=%async_computation.1 | async-start | bytes 262144 | tf_op jit(solution)/shard_map/all_to_all | solution.py:14
  182.3 24.7 %gather_fusion = s32[4096]{0:T(1024)S(1)} fusion(s32[128]{0:T(128)S(1)} %bitcast.3973, s32[4096]{0:T(1024)S(1)} %broadcast_clamp_fusion), kind=kCustom, calls=%fused_computation | custom fusion | bytes 49152 | tf_op jit(solution)/shard_map/jit(_take)/gather | solution.py:89
  231.3 10.6 %all-to-all-start = ((bf16[72,128,32]{0,2,1:T(8,128)(2,1)}), bf16[72,128,32]{0,2,1:T(8,128)(2,1)}, u32[]{:S(2)}, u32[]{:S(2)}) async-start(bf16[72,128,32]{0,2,1:T(8,128)(2,1)} %bitcast.6), calls=%async_computation | async-start | bytes 2097152 | tf_op jit(solution)/shard_map/all_to_all | solution.py:92
  251.5 7.5 %all-to-all-done = bf16[72,128,32]{0,2,1:T(8,128)(2,1)} async-done(((bf16[72,128,32]{0,2,1:T(8,128)(2,1)}), bf16[72,128,32]{0,2,1:T(8,128)(2,1)}, u32[]{:S(2)}, u32[]{:S(2)}) %all-to-all-start) | async-done | bytes 589856 | tf_op jit(solution)/shard_map/all_to_all | solution.py:92
  259.0 13.3 %fusion.3 = f32[72,32,128]{2,0,1:T(8,128)S(1)} fusion(bf16[72,4096,1]{0,1,2:T(8,128)(2,1)} %bitcast.8, s32[32,128]{1,0:T(8,128)} %multiply_add_fusion.4, s32[4096]{0:T(1024)} %param.16, bf16[4096]{0:T(1024)(128)(2,1)} %mul.20172), kind=kOutput, calls=%fused_computation.8 | convolution fusion | flops 2449473536 | bytes 1810432 | tf_op jit(solution)/shard_map/dot_general | solution.py:100
  272.4 13.1 %fusion.2 = f32[72,32,128]{2,0,1:T(8,128)S(1)} fusion(bf16[72,4096,1]{0,1,2:T(8,128)(2,1)} %bitcast.8, s32[32,128]{1,0:T(8,128)S(1)} %copy-done.212, s32[4096]{0:T(1024)S(1)} %copy-done.216, bf16[4096]{0:T(1024)(128)(2,1)S(1)} %copy-done.213), kind=kOutput, calls=%fused_computation.7 | convolution fusion | flops 2449473536 | bytes 1810432 | tf_op jit(solution)/shard_map/dot_general | solution.py:100
  285.5 13.3 %fusion.1 = f32[72,32,128]{2,0,1:T(8,128)S(1)} fusion(bf16[72,4096,1]{0,1,2:T(8,128)(2,1)} %bitcast.8, s32[32,128]{1,0:T(8,128)S(1)} %copy-done.212, s32[4096]{0:T(1024)S(1)} %copy-done.216, bf16[4096]{0:T(1024)(128)(2,1)S(1)} %copy-done.214), kind=kOutput, calls=%fused_computation.6 | convolution fusion | flops 2449473536 | bytes 1810432 | tf_op jit(solution)/shard_map/dot_general | solution.py:100
  298.9 13.2 %fusion = f32[72,32,128]{2,0,1:T(8,128)S(1)} fusion(bf16[72,4096,1]{0,1,2:T(8,128)(2,1)} %bitcast.8, s32[32,128]{1,0:T(8,128)S(1)} %copy-done.212, s32[4096]{0:T(1024)S(1)} %copy-done.216, bf16[4096]{0:T(1024)(128)(2,1)S(1)} %mul.20163), kind=kOutput, calls=%fused_computation.5 | convolution fusion | flops 2449473536 | bytes 1810432 | tf_op jit(solution)/shard_map/dot_general | solution.py:100
  326.3 6.4 %multiply_add_fusion.3 = f32[4,72,32,128]{3,2,0,1:T(8,128)S(1)} fusion(f32[4,72,32,128]{3,2,0,1:T(8,128)S(1)} %maximum_add_fusion, f32[4,72,3,128]{3,2,0,1:T(4,128)S(1)} %copy.2394, f32[4,72,3,128]{3,2,0,1:T(4,128)S(1)} %copy.2396, f32[72,32,128]{2,1,0:T(8,128)S(1)} %multiply_multiply_fusion.1, f32[72,32,128]{2,1,0:T(8,128)S(1)} %copy-done.6), kind=kLoop, calls=%fused_computation.94 | loop fusion | flops 33030144 | bytes 12681216 | tf_op jit(solution)/shard_map/add | solution.py:46
  332.7 5.4 fusion.559
  352.4 8.2 %collective-permute-done.3 = f32[4,72,32,3]{1,2,3,0:T(8,128)S(1)} collective-permute-done((f32[4,72,32,3]{1,2,3,0:T(8,128)S(1)}, f32[4,72,32,3]{1,2,3,0:T(8,128)S(1)}, u32[]{:S(2)}, u32[]{:S(2)}) %collective-permute-start.3) | collective-permute-done | bytes 110624 | tf_op jit(solution)/shard_map/ppermute | solution.py:26
  360.6 5.0 copy.2400
  365.6 5.1 copy.2398
  371.1 32.6 %multiply_add_fusion.2 = f32[4,72,32,128]{3,2,0,1:T(8,128)S(1)} fusion(f32[4,72,32,128]{3,2,0,1:T(8,128)} %copy-done.3, f32[4,72,32,3]{3,2,0,1:T(8,128)} %copy.2398, f32[4,72,32,3]{3,2,0,1:T(8,128)} %copy.2400, f32[72,32,128]{2,1,0:T(8,128)S(1)} %copy-done.11, f32[72,32,128]{2,1,0:T(8,128)S(1)} %copy-done.9), kind=kLoop, calls=%fused_computation.93 | loop fusion | flops 33030144 | bytes 12017664 | tf_op jit(solution)/shard_map/add | solution.py:46
  429.1 6.9 %collective-permute-done.5 = f32[4,72,3,128]{3,1,2,0:T(8,128)S(1)} collective-permute-done((f32[4,72,3,128]{3,1,2,0:T(8,128)S(1)}, f32[4,72,3,128]{3,1,2,0:T(8,128)S(1)}, u32[]{:S(2)}, u32[]{:S(2)}) %collective-permute-start.5) | collective-permute-done | bytes 442400 | tf_op jit(solution)/shard_map/ppermute | solution.py:26
  436.4 22.3 %add_multiply_fusion.5 = (f32[4,72,32,128]{3,2,0,1:T(8,128)}, f32[4,72,32,128]{3,2,0,1:T(8,128)}, f32[4,72,32,128]{3,2,0,1:T(8,128)}, f32[4,72,32,128]{3,2,0,1:T(8,128)}) fusion(f32[4,72,35,128]{3,2,0,1:T(8,128)S(1)} %copy_dynamic-update-slice_fusion, f32[4,72,32,128]{3,2,0,1:T(8,128)} %get-tuple-element.309, f32[4,72,3,128]{3,2,0,1:T(4,128)S(1)} %copy.2508, ...), kind=kLoop, calls=%fused_computation.91 | loop fusion | flops 24772608 | bytes 39370752 | tf_op jit(solution)/shard_map/mul | solution.py:42
  458.7 9.6 %copy_add_fusion.4 = f32[4,72,32,128]{3,2,1,0:T(8,128)S(1)} fusion(f32[4,72,32,128]{3,2,0,1:T(8,128)} %get-tuple-element.302, f32[4,72,32,128]{3,2,0,1:T(8,128)} %get-tuple-element.301, f32[4,72,32,128]{3,2,0,1:T(8,128)} %get-tuple-element.303, f32[4,72,32,128]{3,2,0,1:T(8,128)} %get-tuple-element.300, f32[4,72,32,128]{3,2,1,0:T(8,128)} %copy-done.4, ...), kind=kLoop, calls=%fused_computation.80 | loop fusion | flops 7077888 | bytes 29491200 | tf_op jit(solution)/shard_map/add | solution.py:46
  468.3 5.4 fusion.557
  483.6 7.5 %collective-permute-start.6 = (f32[4,72,32,3]{1,2,3,0:T(8,128)S(1)}, f32[4,72,32,3]{1,2,3,0:T(8,128)S(1)}, u32[]{:S(2)}, u32[]{:S(2)}) collective-permute-start(f32[4,72,32,3]{1,2,3,0:T(8,128)S(1)} %copy.2517), channel_id=1, source_target_pairs={{1,0},{2,1},{3,2},{4,3},{5,4},{6,5},{7,6},{9,8},{10,9},{11,10},{12... | collective-permute-start | bytes 331784 | tf_op jit(solution)/shard_map/ppermute | solution.py:28
  491.2 5.2 copy.2523
  496.4 5.2 copy.2521
  501.6 4.9 copy.2519
  506.6 45.7 %add_multiply_fusion.2 = (f32[4,72,32,128]{3,2,0,1:T(8,128)}, f32[4,72,32,128]{3,2,0,1:T(8,128)}, f32[4,72,32,128]{3,2,0,1:T(8,128)}) fusion(f32[4,72,32,3]{3,2,0,1:T(8,128)} %copy.2519, f32[4,72,32,128]{3,2,0,1:T(8,128)} %copy.2523, f32[4,72,32,3]{3,2,0,1:T(8,128)} %copy.2521, f32[72,32,128]{2,1,0:T(8,128)S(1)} %copy-done.10), kind=kLoop, calls=%fused_computation.87 | loop fusion | flops 25952256 | bytes 20275200 | tf_op jit(solution)/shard_map/mul | solution.py:42
  552.7 11.0 %copy_add_fusion = f32[4,72,32,128]{3,2,1,0:T(8,128)S(1)} fusion(f32[4,72,32,128]{3,2,0,1:T(8,128)} %get-tuple-element.298, f32[4,72,32,128]{3,2,0,1:T(8,128)} %get-tuple-element.299, f32[4,72,32,128]{3,2,0,1:T(8,128)} %get-tuple-element.297, f32[4,72,32,128]{3,2,1,0:T(8,128)S(1)} %bitcast.3975, f32[72,32,128]{2,1,0:T(8,128)S(1)} %copy-done.12, ...), kind=kLoop, calls=%fused_computation.75 | loop fusion | flops 11796480 | bytes 29712384 | tf_op jit(solution)/shard_map/add | solution.py:46
  (806 shorter events, 286.6 us)
Async XLA Ops:
  0.6 181.6 %copy-start = (s32[1,128]{1,0:T(1,128)S(1)}, s32[1,128]{1,0:T(1,128)}, u32[]{:S(2)}) copy-start(s32[1,128]{1,0:T(1,128)} %param.17) | copy-start | bytes 1540
  167.6 63.8 %all-to-all-start.1 = ((bf16[128,4,32]{2,1,0:T(4,128)(2,1)}), bf16[128,4,32]{2,1,0:T(4,128)(2,1)S(1)}, u32[]{:S(2)}, u32[]{:S(2)}) async-start(bf16[128,4,32]{2,1,0:T(4,128)(2,1)} %constant_dynamic-update-slice_fusion), calls=%async_computation.1 | async-start | bytes 262144 | tf_op jit(solution)/shard_map/all_to_all | solution.py:14
  181.4 42.6 %copy-start.50 = (f32[32,128]{1,0:T(8,128)}, f32[32,128]{1,0:T(8,128)S(1)}, u32[]{:S(2)}) copy-start(f32[32,128]{1,0:T(8,128)S(1)} %get-tuple-element.205) | copy-start | bytes 49156
  231.3 27.7 %all-to-all-start = ((bf16[72,128,32]{0,2,1:T(8,128)(2,1)}), bf16[72,128,32]{0,2,1:T(8,128)(2,1)}, u32[]{:S(2)}, u32[]{:S(2)}) async-start(bf16[72,128,32]{0,2,1:T(8,128)(2,1)} %bitcast.6), calls=%async_computation | async-start | bytes 2097152 | tf_op jit(solution)/shard_map/all_to_all | solution.py:92
  243.3 82.9 %copy-start.7 = (f32[72,32,128]{2,1,0:T(8,128)}, f32[72,32,128]{2,1,0:T(8,128)S(1)}, u32[]{:S(2)}) copy-start(f32[72,32,128]{2,1,0:T(8,128)S(1)} %multiply_multiply_fusion.1) | copy-start | bytes 3538948
  314.8 7.1 %collective-permute-start = (f32[4,72,3,128]{3,1,2,0:T(8,128)S(1)}, f32[4,72,3,128]{3,1,2,0:T(8,128)S(1)}, u32[]{:S(2)}, u32[]{:S(2)}) collective-permute-start(f32[4,72,3,128]{3,1,2,0:T(8,128)S(1)} %copy.2393), channel_id=1, source_target_pairs={{8,0},{16,8},{24,16},{32,24},{40,32},{48,40},{56,48},{64,56},{72,6... | collective-permute-start | bytes 1327112 | tf_op jit(solution)/shard_map/ppermute | solution.py:28
  316.1 10.0 %collective-permute-start.1 = (f32[4,72,3,128]{3,1,2,0:T(8,128)S(1)}, f32[4,72,3,128]{3,1,2,0:T(8,128)S(1)}, u32[]{:S(2)}, u32[]{:S(2)}) collective-permute-start(f32[4,72,3,128]{3,1,2,0:T(8,128)S(1)} %copy.2395), channel_id=1, source_target_pairs={{0,8},{8,16},{16,24},{24,32},{32,40},{40,48},{48,56},{56,64},{64,7... | collective-permute-start | bytes 1327112 | tf_op jit(solution)/shard_map/ppermute | solution.py:26
  346.1 19.5 %collective-permute-start.2 = (f32[4,72,32,3]{1,2,3,0:T(8,128)S(1)}, f32[4,72,32,3]{1,2,3,0:T(8,128)S(1)}, u32[]{:S(2)}, u32[]{:S(2)}) collective-permute-start(f32[4,72,32,3]{1,2,3,0:T(8,128)S(1)} %copy.2397), channel_id=1, source_target_pairs={{1,0},{2,1},{3,2},{4,3},{5,4},{6,5},{7,6},{9,8},{10,9},{11,10},{12... | collective-permute-start | bytes 331784 | tf_op jit(solution)/shard_map/ppermute | solution.py:28
  349.4 11.2 %collective-permute-start.3 = (f32[4,72,32,3]{1,2,3,0:T(8,128)S(1)}, f32[4,72,32,3]{1,2,3,0:T(8,128)S(1)}, u32[]{:S(2)}, u32[]{:S(2)}) collective-permute-start(f32[4,72,32,3]{1,2,3,0:T(8,128)S(1)} %copy.2399), channel_id=1, source_target_pairs={{0,1},{1,2},{2,3},{3,4},{4,5},{5,6},{6,7},{8,9},{9,10},{10,11},{11... | collective-permute-start | bytes 331784 | tf_op jit(solution)/shard_map/ppermute | solution.py:26
  352.3 51.3 %copy-start.204 = (f32[32,128]{1,0:T(8,128)}, f32[32,128]{1,0:T(8,128)S(1)}, u32[]{:S(2)}) copy-start(f32[32,128]{1,0:T(8,128)S(1)} %get-tuple-element.507) | copy-start | bytes 49156
  352.3 53.5 %copy-start.192 = (f32[32,128]{1,0:T(8,128)}, f32[32,128]{1,0:T(8,128)S(1)}, u32[]{:S(2)}) copy-start(f32[32,128]{1,0:T(8,128)S(1)} %get-tuple-element.508) | copy-start | bytes 49156
  352.3 53.5 %copy-start.202 = (f32[32,128]{1,0:T(8,128)}, f32[32,128]{1,0:T(8,128)S(1)}, u32[]{:S(2)}) copy-start(f32[32,128]{1,0:T(8,128)S(1)} %get-tuple-element.360) | copy-start | bytes 49156
  352.3 53.5 %copy-start.203 = (f32[32,128]{1,0:T(8,128)}, f32[32,128]{1,0:T(8,128)S(1)}, u32[]{:S(2)}) copy-start(f32[32,128]{1,0:T(8,128)S(1)} %get-tuple-element.506) | copy-start | bytes 49156
  352.4 60.7 %copy-start.135 = (f32[32,128]{1,0:T(8,128)}, f32[32,128]{1,0:T(8,128)S(1)}, u32[]{:S(2)}) copy-start(f32[32,128]{1,0:T(8,128)S(1)} %get-tuple-element.361) | copy-start | bytes 49156
  352.4 60.7 %copy-start.137 = (f32[32,128]{1,0:T(8,128)}, f32[32,128]{1,0:T(8,128)S(1)}, u32[]{:S(2)}) copy-start(f32[32,128]{1,0:T(8,128)S(1)} %get-tuple-element.505) | copy-start | bytes 49156
  370.7 33.0 %copy-start.19 = (f32[1,32,128]{2,1,0:T(8,128)S(1)}, f32[1,32,128]{2,1,0:T(8,128)}, u32[]{:S(2)}) copy-start(f32[1,32,128]{2,1,0:T(8,128)} %copy-done.18) | copy-start | bytes 49156
  370.7 33.0 %copy-start.21 = (f32[1,32,128]{2,1,0:T(8,128)S(1)}, f32[1,32,128]{2,1,0:T(8,128)}, u32[]{:S(2)}) copy-start(f32[1,32,128]{2,1,0:T(8,128)} %copy-done.20) | copy-start | bytes 49156
  424.9 11.3 %collective-permute-start.4 = (f32[4,72,3,128]{3,1,2,0:T(8,128)S(1)}, f32[4,72,3,128]{3,1,2,0:T(8,128)S(1)}, u32[]{:S(2)}, u32[]{:S(2)}) collective-permute-start(f32[4,72,3,128]{3,1,2,0:T(8,128)S(1)} %copy.2504), channel_id=1, source_target_pairs={{8,0},{16,8},{24,16},{32,24},{40,32},{48,40},{56,48},{64,56},{72,6... | collective-permute-start | bytes 1327112 | tf_op jit(solution)/shard_map/ppermute | solution.py:28
  426.1 9.8 %collective-permute-start.5 = (f32[4,72,3,128]{3,1,2,0:T(8,128)S(1)}, f32[4,72,3,128]{3,1,2,0:T(8,128)S(1)}, u32[]{:S(2)}, u32[]{:S(2)}) collective-permute-start(f32[4,72,3,128]{3,1,2,0:T(8,128)S(1)} %copy.2507), channel_id=1, source_target_pairs={{0,8},{8,16},{16,24},{24,32},{32,40},{40,48},{48,56},{56,64},{64,7... | collective-permute-start | bytes 1327112 | tf_op jit(solution)/shard_map/ppermute | solution.py:26
  477.7 18.7 %collective-permute-start.7 = (f32[4,72,32,3]{1,2,3,0:T(8,128)S(1)}, f32[4,72,32,3]{1,2,3,0:T(8,128)S(1)}, u32[]{:S(2)}, u32[]{:S(2)}) collective-permute-start(f32[4,72,32,3]{1,2,3,0:T(8,128)S(1)} %copy.2520), channel_id=1, source_target_pairs={{0,1},{1,2},{2,3},{3,4},{4,5},{5,6},{6,7},{8,9},{9,10},{10,11},{11... | collective-permute-start | bytes 331784 | tf_op jit(solution)/shard_map/ppermute | solution.py:26
  483.6 18.0 %collective-permute-start.6 = (f32[4,72,32,3]{1,2,3,0:T(8,128)S(1)}, f32[4,72,32,3]{1,2,3,0:T(8,128)S(1)}, u32[]{:S(2)}, u32[]{:S(2)}) collective-permute-start(f32[4,72,32,3]{1,2,3,0:T(8,128)S(1)} %copy.2517), channel_id=1, source_target_pairs={{1,0},{2,1},{3,2},{4,3},{5,4},{6,5},{7,6},{9,8},{10,9},{11,10},{12... | collective-permute-start | bytes 331784 | tf_op jit(solution)/shard_map/ppermute | solution.py:28
  501.6 50.7 %slice-start = ((s8[4718592]{0:T(1024)(128)(4,1)}), s8[524288]{0:T(1024)(128)(4,1)S(1)}, s32[]{:S(2)}) async-start(s8[4718592]{0:T(1024)(128)(4,1)} %bitcast.3974), calls=%async_computation.2 | async-start | bytes 1048576
  506.6 45.7 %slice-start.1 = ((s8[4718592]{0:T(1024)(128)(4,1)}), s8[4194304]{0:T(1024)(128)(4,1)S(1)}, s32[]{:S(2)}) async-start(s8[4718592]{0:T(1024)(128)(4,1)} %bitcast.3974), calls=%async_computation.3 | async-start | bytes 8388608
  506.6 45.7 %copy-start.12 = (f32[72,32,128]{2,1,0:T(8,128)S(1)}, f32[72,32,128]{2,1,0:T(8,128)}, u32[]{:S(2)}) copy-start(f32[72,32,128]{2,1,0:T(8,128)} %multiply_multiply_fusion) | copy-start | bytes 3538948
  (207 other events, 2725.3 us)
